TPU v7x, 512 devices: a whole 4x8x8 slice. The times are simulated.
512 devices in a mesh: rep: 64 (over y, z), ctx: 8 (over x, core).
Axes of the slice: x: 4, y: 8, z: 8, core: 2. Of those that a mesh axis runs over, the one named last changes fastest.
Arguments:
- cache_latent: bfloat16 [256, 96, 64, 512], P('rep', 'ctx'), may hold values from -6 to 6
- cache_rope: bfloat16 [256, 96, 4096], P('rep', 'ctx'), may hold values from -6 to 6
- lengths: int32 [256], P('rep'), may hold values from 64 to 6144, as said below
- move_slots: int32 [64, 2], P('rep'), may hold values from 0 to 3, as said below
- q_latent: bfloat16 [256, 2, 128, 512], P('rep'), may hold values from -8 to 8
- q_rope: bfloat16 [256, 2, 8192], P('rep'), may hold values from -8 to 8
- new_keys: bfloat16 [256, 2, 576], P('rep'), may hold values from -6 to 6
Outputs:
- attended: bfloat16 [256, 2, 128, 512], P('rep', None, 'ctx')
Inputs may be any that keep to these rules, and one draw needn't show every extreme that they name: `lengths`: requests of replicas 64/2 and up hold 3072 or more tokens, the others 6144/2 or fewer; the last request holds exactly 6144. `move_slots`: each row lists 2 different slots.
All inputs are finite; a program needn't handle non-finite values.
Results may differ from a plain program's by a relative error of at most 0.005.
Values may be sent and summed in bfloat16 or wider, within the bound.
A program may use at most 64 MiB of HBM per device.

v0:
```python
import jax
import jax.numpy as jnp
from jax import lax
from jax.sharding import PartitionSpec as P

score_scale = 192.0 ** (-0.5)
masked = -1e30


def partner(x, axis, stride):
    return lax.ppermute(x, axis, [(i, i ^ 1 << stride) for i in range(lax.axis_size(axis))])


def local_attention(cache_latent, cache_rope, lengths, q_latent, q_rope, new_keys, group):
    requests, pages, page_len, width = cache_latent.shape
    steps = q_latent.shape[1]
    heads = q_latent.shape[2]
    rot_width = new_keys.shape[2] - width
    span = pages * page_len
    keys = cache_latent.reshape(requests, span, width)
    rotary = cache_rope.reshape(requests, span, rot_width)
    q_rot = q_rope.reshape(requests, steps, heads, rot_width)
    fresh_lat = new_keys[:, :, :width]
    fresh_rot = new_keys[:, :, width:]
    score = (
        jnp.einsum("rshd,rtd->rsht", q_latent, keys, preferred_element_type=jnp.float32)
        + jnp.einsum("rshe,rte->rsht", q_rot, rotary, preferred_element_type=jnp.float32)
    ) * score_scale
    new_score = (
        jnp.einsum("rshd,rnd->rshn", q_latent, fresh_lat, preferred_element_type=jnp.float32)
        + jnp.einsum("rshe,rne->rshn", q_rot, fresh_rot, preferred_element_type=jnp.float32)
    ) * score_scale
    position = group * span + jnp.arange(span, dtype=jnp.int32)
    valid = (position[None, :] < lengths[:, None])[:, None, None, :]
    step_ids = jnp.arange(steps, dtype=jnp.int32)
    new_valid = (step_ids[None, :] <= step_ids[:, None])[None, :, None, :] & (group == 0)
    cache_top = jnp.max(jnp.where(valid, score, masked), axis=-1)
    new_top = jnp.max(jnp.where(new_valid, new_score, masked), axis=-1)
    top = jnp.maximum(cache_top, new_top)
    weights = jnp.where(valid, jnp.exp(score - top[..., None]), 0.0)
    new_weights = jnp.where(new_valid, jnp.exp(new_score - top[..., None]), 0.0)
    totals = jnp.sum(weights, axis=-1) + jnp.sum(new_weights, axis=-1)
    partial_value = jnp.einsum(
        "rsht,rtd->rshd", weights.astype(jnp.bfloat16), keys, preferred_element_type=jnp.float32
    ) + jnp.einsum(
        "rshn,rnd->rshd",
        new_weights.astype(jnp.bfloat16),
        fresh_lat,
        preferred_element_type=jnp.float32,
    )
    return (partial_value.astype(jnp.bfloat16), top, totals)


def merge_groups(partial_value, top, totals):
    parts = lax.all_to_all(partial_value[None], "ctx", split_axis=3, concat_axis=0, tiled=True)
    tops, sums = (
        lax.all_to_all(top[None], "ctx", split_axis=3, concat_axis=0, tiled=True),
        lax.all_to_all(totals[None], "ctx", split_axis=3, concat_axis=0, tiled=True),
    )
    overall = jnp.max(tops, axis=0)
    factor = jnp.exp(tops - overall)
    numer = jnp.sum(factor[..., None] * parts.astype(jnp.float32), axis=0)
    denom = jnp.sum(factor * sums, axis=0)
    return (numer / denom[..., None]).astype(jnp.bfloat16)


def body(cache_latent, cache_rope, lengths, move_slots, q_latent, q_rope, new_keys):
    slots = move_slots[0]
    partner_bit = lax.axis_size("rep").bit_length() - 2
    group = lax.axis_index("ctx")
    got_latent, got_rope, got_lengths = partner(
        (cache_latent[slots], cache_rope[slots], lengths[slots]), "rep", partner_bit
    )
    here_latent = cache_latent.at[slots].set(got_latent)
    here_rope = cache_rope.at[slots].set(got_rope)
    here_lengths = lengths.at[slots].set(got_lengths)
    partial_value, top, totals = local_attention(
        here_latent, here_rope, here_lengths, q_latent, q_rope, new_keys, group
    )
    return merge_groups(partial_value, top, totals)


def solution(mesh):
    in_specs = (
        P("rep", "ctx", None, None),
        P("rep", "ctx", None),
        P("rep"),
        P("rep", None),
        P("rep", None, None, None),
        P("rep", None, None),
        P("rep", None, None),
    )
    out_specs = P("rep", None, "ctx", None)
    return jax.shard_map(body, mesh=mesh, in_specs=in_specs, out_specs=out_specs, check_vma=False)
```

profile of v0, /device:TPU:1, one launch (start us, length us, event | category | flops | bytes accessed | tf_op | source)
XLA Modules:
  0.0 153.3 jit_solution(3932355933455460123)
XLA Ops:
  0.0 4.0 %copy.65 = bf16[4,12,64,512]{3,2,1,0:T(8,128)(2,1)} copy(bf16[4,12,64,512]{3,2,1,0:T(8,128)(2,1)} %param.7) | data formatting | bytes 6291456
  4.3 3.8 %gather_fusion.1 = bf16[2,12,64,512]{3,2,1,0:T(8,128)(2,1)} fusion(bf16[4,12,64,512]{3,2,1,0:T(8,128)(2,1)} %copy.65, s32[1024]{0:T(1024)S(1)} %pad_clamp_fusion), kind=kCustom, calls=%fused_computation.1 | custom fusion | bytes 3145736 | tf_op jit(solution)/shard_map/gather | solution.py:72
  8.1 8.3 %collective-permute-start.1 = (bf16[2,12,64,512]{3,2,1,0:T(8,128)(2,1)}, bf16[2,12,64,512]{3,2,1,0:T(8,128)(2,1)}, u32[]{:S(2)}, u32[]{:S(2)}) collective-permute-start(bf16[2,12,64,512]{3,2,1,0:T(8,128)(2,1)} %gather_fusion.1), channel_id=1, source_target_pairs={{0,256},{8,264},{16,272},{24,280},{32,288},{40,296},{48,304},{56,3... | collective-permute-start | bytes 4718600 | tf_op jit(solution)/shard_map/ppermute | solution.py:11
  17.0 1.9 %collective-permute-start = (s32[2]{0:T(128)S(1)}, s32[2]{0:T(128)S(1)}, u32[]{:S(2)}, u32[]{:S(2)}) collective-permute-start(s32[2]{0:T(128)S(1)} %gather_fusion), channel_id=1, source_target_pairs={{0,256},{8,264},{16,272},{24,280},{32,288},{40,296},{48,304},{56,3... | collective-permute-start | bytes 32 | tf_op jit(solution)/shard_map/ppermute | solution.py:11
  18.9 2.1 %gather_fusion.2 = bf16[2,12,4096]{2,0,1:T(2,128)(2,1)S(1)} fusion(bf16[4,12,4096]{2,0,1:T(4,128)(2,1)S(1)} %copy.66, s32[1024]{0:T(1024)S(1)} %pad_clamp_fusion), kind=kCustom, calls=%fused_computation.2 | custom fusion | bytes 393224 | tf_op jit(solution)/shard_map/gather | solution.py:72
  21.0 7.3 %collective-permute-start.2 = (bf16[2,12,4096]{2,0,1:T(2,128)(2,1)S(1)}, bf16[2,12,4096]{2,0,1:T(2,128)(2,1)S(1)}, u32[]{:S(2)}, u32[]{:S(2)}) collective-permute-start(bf16[2,12,4096]{2,0,1:T(2,128)(2,1)S(1)} %gather_fusion.2), channel_id=1, source_target_pairs={{0,256},{8,264},{16,272},{24,280},{32,288},{40,296},{48,304},{56,3... | collective-permute-start | bytes 589832 | tf_op jit(solution)/shard_map/ppermute | solution.py:11
  29.1 42.6 %collective-permute-done = s32[2]{0:T(128)S(1)} collective-permute-done((s32[2]{0:T(128)S(1)}, s32[2]{0:T(128)S(1)}, u32[]{:S(2)}, u32[]{:S(2)}) %collective-permute-start) | collective-permute-done | bytes 40 | tf_op jit(solution)/shard_map/ppermute | solution.py:11
  72.4 6.3 %collective-permute-done.2 = bf16[2,12,4096]{2,0,1:T(2,128)(2,1)S(1)} collective-permute-done((bf16[2,12,4096]{2,0,1:T(2,128)(2,1)S(1)}, bf16[2,12,4096]{2,0,1:T(2,128)(2,1)S(1)}, u32[]{:S(2)}, u32[]{:S(2)}) %collective-permute-start.2) | collective-permute-done | bytes 196640 | tf_op jit(solution)/shard_map/ppermute | solution.py:11
  78.7 2.3 %scatter_fusion.2 = bf16[4,12,4096]{2,0,1:T(4,128)(2,1)S(1)} fusion(bf16[4,12,4096]{2,0,1:T(4,128)(2,1)S(1)} %copy.66, s32[2]{0:T(128)S(1)} %fusion.20, bf16[2,12,4096]{2,0,1:T(2,128)(2,1)S(1)} %collective-permute-done.2), kind=kCustom, calls=%fused_computation.5 | custom fusion | bytes 589832 | tf_op jit(solution)/shard_map/scatter | solution.py:75
  81.2 0.8 reshape.120
  82.1 2.3 %fusion.6 = f32[4,768,2,128]{3,1,2,0:T(8,128)} fusion(bf16[4,2,128,64]{3,2,1,0:T(8,128)(2,1)S(1)} %reshape.121, bf16[4,768,64]{2,1,0:T(8,128)(2,1)S(1)} %reshape.120), kind=kOutput, calls=%fused_computation.20 | convolution fusion | flops 100663296 | bytes 3670016 | tf_op jit(solution)/shard_map/rshe,rte->rsht/dot_general | solution.py:27
  84.3 5.2 %scatter_fusion.1 = bf16[4,12,64,512]{3,2,1,0:T(8,128)(2,1)} fusion(bf16[4,12,64,512]{3,2,1,0:T(8,128)(2,1)} %copy.65, s32[2]{0:T(128)S(1)} %fusion.20, bf16[2,12,64,512]{3,2,1,0:T(8,128)(2,1)} %collective-permute-done.1), kind=kCustom, calls=%fused_computation.4 | custom fusion | bytes 4718600 | tf_op jit(solution)/shard_map/scatter | solution.py:74
  89.5 4.0 %select_reduce_fusion = (f32[4,2,128]{2,1,0:T(2,128)S(1)}, f32[4,768,2,128]{3,1,2,0:T(8,128)S(1)}) fusion(pred[4,768]{1,0:T(4,128)(4,1)S(1)} %broadcast_compare_fusion, f32[4,768,2,128]{3,1,2,0:T(8,128)} %fusion.6, bf16[4,768,512,1]{2,1,3,0:T(8,128)(2,1)} %bitcast.73, bf16[4,2,128,512]{3,2,1,0:T(8,128)(2,1)S(1)} %copy-done), kind=kOutput, calls=%fused_computation.9 | convolution fusion | flops 808451072 | bytes 10492928 | tf_op jit(solution)/shard_map/rshd,rtd->rsht/dot_general | solution.py:26
  93.5 1.7 %copy-done.1 = f32[4,768,2,128]{3,1,2,0:T(8,128)} copy-done((f32[4,768,2,128]{3,1,2,0:T(8,128)}, f32[4,768,2,128]{3,1,2,0:T(8,128)S(1)}, u32[]{:S(2)}) %copy-start.1) | copy-done | bytes 3145752
  96.9 19.6 %all-to-all-start.2 = ((f32[8,1,128]{2,1,0:T(1,128)}), f32[8,1,128]{2,1,0:T(1,128)S(1)}, u32[]{:S(2)}, u32[]{:S(2)}) async-start(f32[8,1,128]{2,1,0:T(1,128)} %reshape.178), calls=%async_computation.2 | async-start | bytes 8192 | tf_op jit(solution)/shard_map/all_to_all | solution.py:58
  118.0 3.0 %all-to-all-done.2 = f32[8,1,128]{2,1,0:T(1,128)S(1)} async-done(((f32[8,1,128]{2,1,0:T(1,128)}), f32[8,1,128]{2,1,0:T(1,128)S(1)}, u32[]{:S(2)}, u32[]{:S(2)}) %all-to-all-start.2) | async-done | bytes 4128 | tf_op jit(solution)/shard_map/all_to_all | solution.py:58
  121.0 3.9 %all-to-all-start = ((f32[8,1,128]{2,1,0:T(1,128)}), f32[8,1,128]{2,1,0:T(1,128)S(1)}, u32[]{:S(2)}, u32[]{:S(2)}) async-start(f32[8,1,128]{2,1,0:T(1,128)} %reshape.176), calls=%async_computation | async-start | bytes 8192 | tf_op jit(solution)/shard_map/all_to_all | solution.py:57
  124.9 4.2 %fusion.4 = bf16[1,4,2,128,512]{4,3,2,1,0:T(8,128)(2,1)S(1)} fusion(f32[4,2,128,512]{3,2,1,0:T(8,128)S(1)} %fusion.11, bf16[4,768,512,1]{2,1,3,0:T(8,128)(2,1)} %bitcast.74, f32[4,768,2,128]{3,1,2,0:T(8,128)} %copy-done.1, f32[4,2,128]{2,1,0:T(2,128)S(1)} %max.17, pred[4,768]{1,0:T(4,128)(4,1)S(1)} %broadcast_compare_fusion), kind=kOutput, calls=%fused_computation.17 | convolution fusion | flops 808714240 | bytes 9444352 | tf_op jit(solution)/shard_map/rsht,rtd->rshd/dot_general | solution.py:43
  129.1 2.1 %copy.42 = bf16[1,4,2,128,512]{4,2,1,0,3:T(2,128)(2,1)} copy(bf16[1,4,2,128,512]{4,3,2,1,0:T(8,128)(2,1)S(1)} %fusion.4) | data formatting | bytes 2097152 | tf_op jit(solution)/shard_map/broadcast_in_dim | solution.py:55
  131.2 4.8 %all-to-all-start.1 = ((bf16[1,4,2,128,512]{4,2,1,0,3:T(2,128)(2,1)}), bf16[1,4,2,128,512]{4,2,1,0,3:T(2,128)(2,1)S(1)}, u32[]{:S(2)}, u32[]{:S(2)}) async-start(bf16[1,4,2,128,512]{4,2,1,0,3:T(2,128)(2,1)} %copy.42), calls=%async_computation.1 | async-start | bytes 2097152 | tf_op jit(solution)/shard_map/all_to_all | solution.py:55
  137.4 0.9 copy.44
  139.2 0.9 copy.40
  140.4 10.7 %all-to-all-done.1 = bf16[1,4,2,128,512]{4,2,1,0,3:T(2,128)(2,1)S(1)} async-done(((bf16[1,4,2,128,512]{4,2,1,0,3:T(2,128)(2,1)}), bf16[1,4,2,128,512]{4,2,1,0,3:T(2,128)(2,1)S(1)}, u32[]{:S(2)}, u32[]{:S(2)}) %all-to-all-start.1) | async-done | bytes 1048608 | tf_op jit(solution)/shard_map/all_to_all | solution.py:55
  151.1 1.4 fusion
  (46 shorter events, 9.2 us)
Async XLA Ops:
  0.0 28.5 %copy-start = (bf16[4,2,128,512]{3,2,1,0:T(8,128)(2,1)S(1)}, bf16[4,2,128,512]{3,2,1,0:T(8,128)(2,1)}, u32[]{:S(2)}) copy-start(bf16[4,2,128,512]{3,2,1,0:T(8,128)(2,1)} %param.11) | copy-start | bytes 3145732
  0.0 4.0 %copy-start.2 = (bf16[4,12,4096]{2,0,1:T(4,128)(2,1)S(1)}, bf16[4,12,4096]{2,0,1:T(4,128)(2,1)}, u32[]{:S(2)}) copy-start(bf16[4,12,4096]{2,0,1:T(4,128)(2,1)} %param.8) | copy-start | bytes 1179652
  0.0 4.0 %copy-start.5 = (s32[4]{0:T(128)S(1)}, s32[4]{0:T(128)}, u32[]{:S(2)}) copy-start(s32[4]{0:T(128)} %param.9) | copy-start | bytes 52
  0.0 4.2 %copy-start.6 = (s32[1,2]{1,0:T(1,128)S(1)}, s32[1,2]{1,0:T(1,128)}, u32[]{:S(2)}) copy-start(s32[1,2]{1,0:T(1,128)} %param.10) | copy-start | bytes 28
  4.2 24.0 %copy-start.3 = (bf16[4,2,8192]{2,1,0:T(2,128)(2,1)S(1)}, bf16[4,2,8192]{2,1,0:T(2,128)(2,1)}, u32[]{:S(2)}) copy-start(bf16[4,2,8192]{2,1,0:T(2,128)(2,1)} %param.12) | copy-start | bytes 393220
  4.3 24.3 %copy-start.4 = (bf16[4,2,576]{2,1,0:T(2,128)(2,1)S(1)}, bf16[4,2,576]{2,1,0:T(2,128)(2,1)}, u32[]{:S(2)}) copy-start(bf16[4,2,576]{2,1,0:T(2,128)(2,1)} %param.13) | copy-start | bytes 27652
  8.1 76.3 %collective-permute-start.1 = (bf16[2,12,64,512]{3,2,1,0:T(8,128)(2,1)}, bf16[2,12,64,512]{3,2,1,0:T(8,128)(2,1)}, u32[]{:S(2)}, u32[]{:S(2)}) collective-permute-start(bf16[2,12,64,512]{3,2,1,0:T(8,128)(2,1)} %gather_fusion.1), channel_id=1, source_target_pairs={{0,256},{8,264},{16,272},{24,280},{32,288},{40,296},{48,304},{56,3... | collective-permute-start | bytes 4718600 | tf_op jit(solution)/shard_map/ppermute | solution.py:11
  17.0 54.7 %collective-permute-start = (s32[2]{0:T(128)S(1)}, s32[2]{0:T(128)S(1)}, u32[]{:S(2)}, u32[]{:S(2)}) collective-permute-start(s32[2]{0:T(128)S(1)} %gather_fusion), channel_id=1, source_target_pairs={{0,256},{8,264},{16,272},{24,280},{32,288},{40,296},{48,304},{56,3... | collective-permute-start | bytes 32 | tf_op jit(solution)/shard_map/ppermute | solution.py:11
  21.0 57.7 %collective-permute-start.2 = (bf16[2,12,4096]{2,0,1:T(2,128)(2,1)S(1)}, bf16[2,12,4096]{2,0,1:T(2,128)(2,1)S(1)}, u32[]{:S(2)}, u32[]{:S(2)}) collective-permute-start(bf16[2,12,4096]{2,0,1:T(2,128)(2,1)S(1)} %gather_fusion.2), channel_id=1, source_target_pairs={{0,256},{8,264},{16,272},{24,280},{32,288},{40,296},{48,304},{56,3... | collective-permute-start | bytes 589832 | tf_op jit(solution)/shard_map/ppermute | solution.py:11
  93.5 1.7 %copy-start.1 = (f32[4,768,2,128]{3,1,2,0:T(8,128)}, f32[4,768,2,128]{3,1,2,0:T(8,128)S(1)}, u32[]{:S(2)}) copy-start(f32[4,768,2,128]{3,1,2,0:T(8,128)S(1)} %get-tuple-element.8) | copy-start | bytes 9437188
  96.9 24.1 %all-to-all-start.2 = ((f32[8,1,128]{2,1,0:T(1,128)}), f32[8,1,128]{2,1,0:T(1,128)S(1)}, u32[]{:S(2)}, u32[]{:S(2)}) async-start(f32[8,1,128]{2,1,0:T(1,128)} %reshape.178), calls=%async_computation.2 | async-start | bytes 8192 | tf_op jit(solution)/shard_map/all_to_all | solution.py:58
  121.0 10.2 %all-to-all-start = ((f32[8,1,128]{2,1,0:T(1,128)}), f32[8,1,128]{2,1,0:T(1,128)S(1)}, u32[]{:S(2)}, u32[]{:S(2)}) async-start(f32[8,1,128]{2,1,0:T(1,128)} %reshape.176), calls=%async_computation | async-start | bytes 8192 | tf_op jit(solution)/shard_map/all_to_all | solution.py:57
  131.2 19.9 %all-to-all-start.1 = ((bf16[1,4,2,128,512]{4,2,1,0,3:T(2,128)(2,1)}), bf16[1,4,2,128,512]{4,2,1,0,3:T(2,128)(2,1)S(1)}, u32[]{:S(2)}, u32[]{:S(2)}) async-start(bf16[1,4,2,128,512]{4,2,1,0,3:T(2,128)(2,1)} %copy.42), calls=%async_computation.1 | async-start | bytes 2097152 | tf_op jit(solution)/shard_map/all_to_all | solution.py:55
where the time goes:
time: 154 us; the launch traced here: 153 us
  waiting for transfers between devices  62.6 us (41%)
  starting transfers between devices  45.7 us (30%)
  local copies, waits for them, and re-layouts  28.5 us (19%)
  matrix products  11.6 us (8%)
  other arithmetic  4.58 us (3%)
    ppermute x3, waiting for transfers between devices, partner(): lax.ppermute(x, axis, [(i, i ^ 1 << stride) for i in range(lax.axis_size(...  48.9 us
    all_to_all x1, starting transfers between devices, merge_groups(): lax.all_to_all(totals[None], 'ctx', split_axis=3, concat_axis=0, tiled=True)  19.6 us
    ppermute x3, starting transfers between devices, partner(): lax.ppermute(x, axis, [(i, i ^ 1 << stride) for i in range(lax.axis_size(...  17.5 us
    all_to_all x1, waiting for transfers between devices, merge_groups(): lax.all_to_all(partial_value[None], 'ctx', split_axis=3, concat_axis=0, t...  10.7 us
    unnamed x21, local copies, waits for them, and re-layouts  7.96 us
    scatter x1, local copies, waits for them, and re-layouts, body(): here_latent = cache_latent.at[slots].set(got_latent)  5.17 us
    all_to_all x1, starting transfers between devices, merge_groups(): lax.all_to_all(partial_value[None], 'ctx', split_axis=3, concat_axis=0, t...  4.82 us
    dot_general x1, matrix products, local_attention(): jnp.einsum('rsht,rtd->rshd', weights.astype(jnp.bfloat16), keys, preferre...  4.22 us
  transfers between devices with their start and end apart: 6, of which 4 were waited for; matrix products, arithmetic and copies ran while one was open for 14% of the time, Pallas kernels for 0%

commit v1 on v0

v1 whole, which is shorter than its diff:
```python
import functools

import jax
import jax.numpy as jnp
import numpy as np
from jax import lax
from jax.experimental import pallas as pl
from jax.experimental.pallas import tpu as pltpu
from jax.sharding import PartitionSpec as P

score_scale = 192.0 ** (-0.5)
masked = -1e30
MESH = pl.DeviceIdType.MESH
F32 = jnp.float32
BF16 = jnp.bfloat16


def nt(a, b):
    return lax.dot_general(a, b, (((1,), (1,)), ((), ())), preferred_element_type=F32)


def nn(a, b):
    return lax.dot_general(a, b, (((1,), (0,)), ((), ())), preferred_element_type=F32)


def iota(shape, dim):
    return lax.broadcasted_iota(jnp.int32, shape, dim)


def spread_heads(pairs):
    n = pairs.shape[0]
    row, col = iota((2 * n, n), 0), iota((2 * n, n), 1)
    pick = jnp.where(col == (row >> 1), 1.0, 0.0).astype(BF16)
    both = nn(pick, pairs)
    row, lane = iota((2 * n, 128), 0), iota((2 * n, 128), 1)
    one = jnp.where((lane >> 6) == (row & 1), both, 0.0)
    return (one + pltpu.roll(one, 64, 1)).astype(BF16)


def stats_block(top, total):
    lane = iota((top.shape[0], 128), 1)
    block = jnp.zeros((top.shape[0], 128), F32)
    for at, value, terms in ((0, top, 3), (3, total, 2)):
        for n in range(terms):
            term = value.astype(BF16).astype(F32)
            block = jnp.where(lane == at + n, term, block)
            value = value - term
    return block.astype(BF16)


def read_stats(block):
    block = block.astype(F32)
    return block[:, 0:1] + block[:, 1:2] + block[:, 2:3], block[:, 3:4] + block[:, 4:5]


def kernel(
    n_rep,
    plan,
    lengths,
    moves,
    lat_hbm,
    rope_hbm,
    q_hbm,
    qr_hbm,
    nk_hbm,
    out,
    lat_v,
    rope_v,
    q_v,
    qown,
    qr_v,
    nk_v,
    xq,
    xk,
    rk,
    nkx,
    nkf,
    msg,
    qall,
    psend,
    precv,
    own,
    ownstat,
    rs,
    rr,
    newp,
    newstat,
    ysend,
    res,
    in_sem,
    y_s,
    y_r,
    ag_s,
    ag_r,
    sb_s,
    sb_r,
    p_s,
    p_r,
    r_s,
    r_r,
    o_s,
    o_r,
):
    rep = lax.axis_index("rep")
    ctx = lax.axis_index("ctx")
    cx = ctx // 2
    core = ctx % 2
    partner = {"rep": (rep + n_rep // 2) % n_rep, "ctx": ctx}
    sibling = {"rep": rep, "ctx": cx * 2 + (1 - core)}

    def chip(d):
        return {"rep": rep, "ctx": ((cx + d) % 4) * 2 + core}

    loads = {}

    def load(name, src, dst):
        copy = pltpu.make_async_copy(src, dst, in_sem.at[len(loads)])
        copy.start()
        loads[name] = copy

    for s in range(2):
        load(("own", s), q_hbm.at[:, s, pl.ds(pl.multiple_of(ctx * 16, 16), 16), :], qown.at[:, s])
    load("qr", qr_hbm, qr_v)
    load("nk", nk_hbm, nk_v)
    load("rope", rope_hbm, rope_v)
    for i in range(4):
        load(("lat", i), lat_hbm.at[i], lat_v.at[i])
    for g in range(8):
        c = (core + g // 4) % 2
        head = pl.multiple_of(((g % 4) * 2 + c) * 16, 16)
        for s in range(2):
            load(("q", g, s), q_hbm.at[:, s, pl.ds(head, 16), :], q_v.at[:, g, s])

    barrier = pltpu.get_barrier_semaphore()
    for peer in (partner, sibling, chip(1), chip(2), chip(3)):
        pl.semaphore_signal(barrier, inc=1, device_id=peer, device_id_type=MESH)

    row = (moves[0, 0] * 4 + moves[0, 1]) * 8
    slots = [plan[row + i] for i in range(4)]
    places = [plan[row + 4 + b] for b in range(4)]

    loads["qr"].wait()
    for i in range(4):
        rows = qr_v[i].astype(F32)
        for b in range(64):
            j = b // 8
            at = ((j % 2) * 4 + j // 2) * 16 + b % 8
            for s in range(2):
                xq[i, at + 8 * s : at + 8 * s + 1, :] = rows[s : s + 1, 128 * b : 128 * b + 128]

    def pairs_of(slot, c):
        return xq[slot, pl.ds(pl.multiple_of(c * 64, 64), 64), :].astype(BF16)

    def own_pairs(slot):
        return xq[slot, pl.ds(pl.multiple_of(core * 64 + cx * 16, 16), 16), :].astype(BF16)

    for name in (("own", 0), ("own", 1), "nk"):
        loads[name].wait()
    nkx[...] = jnp.zeros_like(nkx)
    for k in range(2):
        slot = slots[2 + k]
        msg[k, :, 0:512] = qown[slot].reshape(32, 512)
        msg[k, 0:16, 512:640] = own_pairs(slot)
        fresh = nk_v[slot].astype(F32)
        for n in range(2):
            for u in range(4):
                nkx[n * 4 + u : n * 4 + u + 1, :] = fresh[n : n + 1, 128 * u : 128 * u + 128]
            nkx[8 + n : 9 + n, 0:64] = fresh[n : n + 1, 512:576]
        msg[k, 16:32, 512:640] = nkx[...].astype(BF16)

    pl.semaphore_wait(barrier, 5)
    y_out = []
    for k in range(2):
        copy = pltpu.make_async_remote_copy(
            src_ref=msg.at[k],
            dst_ref=qall.at[k, cx],
            send_sem=y_s.at[k],
            recv_sem=y_r.at[k],
            device_id=partner,
            device_id_type=MESH,
        )
        copy.start()
        y_out.append(copy)

    loads["rope"].wait()
    xk[...] = jnp.zeros_like(xk)
    for i in range(4):
        for c in range(32):
            xk[c * 16 : c * 16 + 12, i * 128 : i * 128 + 128] = rope_v[i, :, c * 128 : c * 128 + 128]
    token, col = iota((768, 512), 0), iota((768, 512), 1)
    pick = jnp.where(col == ((token & 63) >> 1) * 16 + (token >> 6), 1.0, 0.0).astype(BF16)
    keys2 = nn(pick, xk[...])
    token, lane = iota((768, 128), 0), iota((768, 128), 1)
    keep = (lane >> 6) == (token & 1)
    for i in range(4):
        rk[i] = jnp.where(keep, keys2[:, i * 128 : i * 128 + 128], 0.0).astype(BF16)

    for i in range(4):
        loads[("lat", i)].wait()
    for g in range(8):
        for s in range(2):
            loads[("q", g, s)].wait()

    def attend(i, q, pairs):
        slot = slots[i]
        keys = lat_v[slot]
        score = (nt(q, keys) + nt(spread_heads(pairs), rk[slot])) * score_scale
        position = ctx * 768 + iota((1, 768), 1)
        valid = position < lengths[slot]
        score = jnp.where(valid, score, masked)
        top = jnp.max(score, axis=1, keepdims=True)
        weights = jnp.where(valid, jnp.exp(score - top), 0.0)
        total = jnp.sum(weights, axis=1, keepdims=True)
        part = nn(weights.astype(BF16), keys).astype(BF16)
        psend[i, :, 0:512] = part[128:256]
        psend[i, :, 512:640] = stats_block(top[128:256], total[128:256])
        copy = pltpu.make_async_remote_copy(
            src_ref=psend.at[i],
            dst_ref=precv.at[i],
            send_sem=p_s.at[i],
            recv_sem=p_r.at[i],
            device_id=sibling,
            device_id_type=MESH,
        )
        copy.start()
        own[i] = part[0:128]
        lane = iota((128, 128), 1)
        ownstat[i] = jnp.where(lane == 0, top[0:128], total[0:128])
        return copy

    def merge_cores(i, pair):
        pair.wait()
        top_a, total_a = ownstat[i, :, 0:1], ownstat[i, :, 1:2]
        top_b, total_b = read_stats(precv[i, :, 512:640])
        top = jnp.maximum(top_a, top_b)
        scale_a, scale_b = jnp.exp(top_a - top), jnp.exp(top_b - top)
        part = scale_a * own[i].astype(F32) + scale_b * precv[i, :, 0:512].astype(F32)
        rs[i, :, :, 0:512] = part.astype(BF16).reshape(4, 32, 512)
        stats = stats_block(top, scale_a * total_a + scale_b * total_b)
        rs[i, :, :, 512:640] = stats.reshape(4, 32, 128)
        copies = []
        for d in range(1, 4):
            copy = pltpu.make_async_remote_copy(
                src_ref=rs.at[i, (cx + d) % 4],
                dst_ref=rr.at[i, cx],
                send_sem=r_s.at[i, d],
                recv_sem=r_r.at[i, d],
                device_id=chip(d),
                device_id_type=MESH,
            )
            copy.start()
            copies.append(copy)
        rr[i, cx] = rs[i, cx]
        return copies

    def merge_chips(i, copies):
        for copy in copies:
            copy.wait()
        blocks = [rr[i, c] for c in range(4)]
        parts = [b[:, 0:512].astype(F32) for b in blocks] + [newp[i]]
        stats = [read_stats(b[:, 512:640]) for b in blocks]
        stats.append((newstat[i, :, 0:1], newstat[i, :, 1:2]))
        top = functools.reduce(jnp.maximum, [t for t, _ in stats])
        factors = [jnp.exp(t - top) for t, _ in stats]
        numer = sum(f * p for f, p in zip(factors, parts))
        denom = sum(f * t for f, (_, t) in zip(factors, stats))
        return (numer / denom).astype(BF16)

    pairs = [None] * 4
    chips = [None] * 4
    for i in range(2):
        slot = slots[i]
        both = jnp.concatenate([pairs_of(slot, core), pairs_of(slot, 1 - core)], axis=0)
        pairs[i] = attend(i, q_v[slot].reshape(256, 512), both)
    for i in range(2):
        chips[i] = merge_cores(i, pairs[i])

    gathers = []
    passes = []

    def to_sibling(k, d):
        c = (cx - d + 4) % 4
        copy = pltpu.make_async_remote_copy(
            src_ref=qall.at[k, c],
            dst_ref=qall.at[k, 4 + c],
            send_sem=sb_s.at[k, d],
            recv_sem=sb_r.at[k, d],
            device_id=sibling,
            device_id_type=MESH,
        )
        copy.start()
        passes.append((k, copy))

    for k in range(2):
        y_out[k].wait_recv()
        for d in (2, 1, 3):
            copy = pltpu.make_async_remote_copy(
                src_ref=qall.at[k, cx],
                dst_ref=qall.at[k, cx],
                send_sem=ag_s.at[k, d],
                recv_sem=ag_r.at[k, d],
                device_id=chip(d),
                device_id_type=MESH,
            )
            copy.start()
            gathers.append((k, d, copy))
        to_sibling(k, 0)

    nkf[...] = jnp.zeros_like(nkf)
    for i in range(2):
        nkf[2 * i : 2 * i + 2, 0:576] = nk_v[slots[i]].astype(F32)
    for k in range(2):
        fresh = qall[k, cx, 16:32, 512:640].astype(F32)
        for n in range(2):
            at = 4 + 2 * k + n
            for u in range(4):
                nkf[at : at + 1, 128 * u : 128 * u + 128] = fresh[n * 4 + u : n * 4 + u + 1, :]
            nkf[at : at + 1, 512:576] = fresh[8 + n : 9 + n, 0:64]
    fresh = nkf[...].astype(BF16)
    queries = [qown[slots[i]].reshape(32, 512) for i in range(2)] + [qall[k, cx, :, 0:512] for k in range(2)]
    queries = jnp.concatenate(queries, axis=0)
    rot = [own_pairs(slots[i]) for i in range(2)] + [qall[k, cx, 0:16, 512:640] for k in range(2)]
    rot = spread_heads(jnp.concatenate(rot, axis=0))
    score = (nt(queries, fresh[:, 0:512]) + nt(rot, fresh[:, 512:640])) * score_scale
    row, col = iota((128, 128), 0), iota((128, 128), 1)
    valid = ((row >> 5) == (col >> 1)) & ((col & 1) <= ((row >> 4) & 1))
    score = jnp.where(valid, score, masked)
    top = jnp.max(score, axis=1, keepdims=True)
    weights = jnp.where(valid, jnp.exp(score - top), 0.0)
    total = jnp.sum(weights, axis=1, keepdims=True)
    newp[...] = nn(weights.astype(BF16), fresh[:, 0:512]).reshape(4, 32, 512)
    newstat[...] = jnp.where(col == 0, top, total).reshape(4, 32, 128)

    for k, d, copy in gathers:
        copy.wait_recv()
        to_sibling(k, d)

    for k in range(2):
        for kk, copy in passes:
            if kk == k:
                copy.wait_recv()
        rot = qall[k, :, 0:16, 512:640].reshape(128, 128)
        pairs[2 + k] = attend(2 + k, qall[k, :, :, 0:512].reshape(256, 512), rot)
    for k in range(2):
        chips[2 + k] = merge_cores(2 + k, pairs[2 + k])

    for i in range(2):
        res[i] = merge_chips(i, chips[i])
    home = []
    for k in range(2):
        ysend[k] = merge_chips(2 + k, chips[2 + k])
        copy = pltpu.make_async_remote_copy(
            src_ref=ysend.at[k],
            dst_ref=res.at[2 + k],
            send_sem=o_s.at[k],
            recv_sem=o_r.at[k],
            device_id=partner,
            device_id_type=MESH,
        )
        copy.start()
        home.append(copy)

    for copy in y_out:
        copy.wait_send()
    for _, _, copy in gathers:
        copy.wait_send()
    for _, copy in passes:
        copy.wait_send()
    for copy in home:
        copy.wait()

    for b in range(4):
        out[b] = res[places[b]]


def plan_table():
    rows = np.zeros((4, 4, 8), np.int32)
    for first in range(4):
        for second in range(4):
            stay = [b for b in range(4) if b not in (first, second)]
            slots = (stay + [first, second])[:4] if first != second else [0, 1, 2, 3]
            rows[first, second, :4] = slots
            rows[first, second, 4:] = [slots.index(b) for b in range(4)]
    return rows.reshape(128)


def body(cache_latent, cache_rope, lengths, move_slots, q_latent, q_rope, new_keys):
    dma = pltpu.SemaphoreType.DMA
    smem = pl.BlockSpec(memory_space=pltpu.SMEM)
    hbm = pl.BlockSpec(memory_space=pl.ANY)
    out = pl.pallas_call(
        functools.partial(kernel, lax.axis_size("rep")),
        out_shape=jax.ShapeDtypeStruct((4, 32, 512), BF16),
        in_specs=[smem, smem, smem, hbm, hbm, hbm, hbm, hbm],
        out_specs=pl.BlockSpec(memory_space=pltpu.VMEM),
        scratch_shapes=[
            pltpu.VMEM((4, 768, 512), BF16),
            pltpu.VMEM((4, 12, 4096), BF16),
            pltpu.VMEM((4, 8, 2, 16, 512), BF16),
            pltpu.VMEM((4, 2, 16, 512), BF16),
            pltpu.VMEM((4, 2, 8192), BF16),
            pltpu.VMEM((4, 2, 576), BF16),
            pltpu.VMEM((4, 128, 128), F32),
            pltpu.VMEM((512, 512), BF16),
            pltpu.VMEM((4, 768, 128), BF16),
            pltpu.VMEM((16, 128), F32),
            pltpu.VMEM((128, 640), F32),
            pltpu.VMEM((2, 32, 640), BF16),
            pltpu.VMEM((2, 8, 32, 640), BF16),
            pltpu.VMEM((4, 128, 640), BF16),
            pltpu.VMEM((4, 128, 640), BF16),
            pltpu.VMEM((4, 128, 512), BF16),
            pltpu.VMEM((4, 128, 128), F32),
            pltpu.VMEM((4, 4, 32, 640), BF16),
            pltpu.VMEM((4, 4, 32, 640), BF16),
            pltpu.VMEM((4, 32, 512), F32),
            pltpu.VMEM((4, 32, 128), F32),
            pltpu.VMEM((2, 32, 512), BF16),
            pltpu.VMEM((4, 32, 512), BF16),
            dma((32,)),
            dma((2,)),
            dma((2,)),
            dma((2, 4)),
            dma((2, 4)),
            dma((2, 4)),
            dma((2, 4)),
            dma((4,)),
            dma((4,)),
            dma((4, 4)),
            dma((4, 4)),
            dma((2,)),
            dma((2,)),
        ],
        compiler_params=pltpu.CompilerParams(
            collective_id=0, has_side_effects=True, vmem_limit_bytes=48 * 1024 * 1024
        ),
        cost_estimate=pl.CostEstimate(flops=1800000000, bytes_accessed=4800000, transcendentals=800000),
    )(
        jnp.asarray(plan_table()),
        lengths,
        move_slots,
        cache_latent.reshape(4, 768, 512),
        cache_rope,
        q_latent,
        q_rope,
        new_keys,
    )
    return out.reshape(4, 2, 16, 512)


def solution(mesh):
    in_specs = (
        P("rep", "ctx", None, None),
        P("rep", "ctx", None),
        P("rep"),
        P("rep", None),
        P("rep", None, None, None),
        P("rep", None, None),
        P("rep", None, None),
    )
    out_specs = P("rep", None, "ctx", None)
    return jax.shard_map(body, mesh=mesh, in_specs=in_specs, out_specs=out_specs, check_vma=False)
```

time: 154 us -> 48.1 us (0.31)
  waiting for transfers between devices: 62.6 us -> 0 us
  starting transfers between devices: 45.7 us -> 0 us
  Pallas kernels: 0 us -> 39.2 us
  local copies, waits for them, and re-layouts: 28.5 us -> 8.56 us
  matrix products: 11.6 us -> 0 us
  other arithmetic: 4.58 us -> 0 us
    ppermute x3 -> x0, waiting for transfers between devices: 48.9 us -> none  [partner(): lax.ppermute(x, axis, [(i, i ^ 1 << stride) for i in range(lax.axis_size(...]
    pallas_call x0 -> x1, Pallas kernels: none -> 39.2 us  [body(): pl.pallas_call(functools.partial(kernel, lax.axis_size('rep')), out_shape...]
    all_to_all x3 -> x0, starting transfers between devices: 28.3 us -> none  [the longest x1 19.6 us: merge_groups(): lax.all_to_all(totals[None], 'ctx', split_axis=3, concat_axis=0, tiled=True)]
    ppermute x3 -> x0, starting transfers between devices: 17.5 us -> none  [partner(): lax.ppermute(x, axis, [(i, i ^ 1 << stride) for i in range(lax.axis_size(...]
    all_to_all x3 -> x0, waiting for transfers between devices: 13.7 us -> none  [the longest x1 10.7 us: merge_groups(): lax.all_to_all(partial_value[None], 'ctx', split_axis=3, concat_axis=0, t...]
    dot_general x6 -> x0, matrix products: 11.6 us -> none  [the longest x1 4.22 us: local_attention(): jnp.einsum('rsht,rtd->rshd', weights.astype(jnp.bfloat16), keys, preferre...]
    scatter x4 -> x0, local copies, waits for them, and re-layouts: 8.3 us -> none  [the longest x1 5.17 us: body(): here_latent = cache_latent.at[slots].set(got_latent)]
    gather x3 -> x0, local copies, waits for them, and re-layouts: 6.49 us -> none  [the longest x1 3.8 us: body(): cache_latent[slots]]
  transfers between devices with their start and end apart: 6 -> 0, of which waited for: 4 -> 0; matrix products, arithmetic and copies ran while one was open for 14% -> 0% of each run, Pallas kernels for 0% -> 0%
where the time goes in v1:
time: 48.1 us; the launch traced here: 47.8 us
  Pallas kernels  39.2 us (81%)
  local copies, waits for them, and re-layouts  8.56 us (18%)
    pallas_call x1, Pallas kernels, body(): pl.pallas_call(functools.partial(kernel, lax.axis_size('rep')), out_shape...  39.2 us
    unnamed x16, local copies, waits for them, and re-layouts  8.56 us

profile of v1, /device:TPU:1, one launch (start us, length us, event | category | flops | bytes accessed | tf_op | source)
XLA Modules:
  0.0 47.8 jit_solution(6036702827573828652)
XLA Ops:
  0.0 1.2 %copy.9.rope_hbm = bf16[4,12,4096]{2,1,0:T(8,128)(2,1)S(1)} copy(bf16[4,12,4096]{2,0,1:T(4,128)(2,1)} %param.9) | data formatting | bytes 786432 | tf_op args[1]
  1.2 0.0 copy-start
  1.2 1.9 %copy-done = bf16[4,12,64,512]{3,2,1,0:T(8,128)(2,1)S(1)} copy-done((bf16[4,12,64,512]{3,2,1,0:T(8,128)(2,1)S(1)}, bf16[4,12,64,512]{3,2,1,0:T(8,128)(2,1)}, u32[]{:S(2)}) %copy-start) | copy-done | bytes 3145752
  3.1 0.0 copy-start.1
  3.1 1.2 %copy-done.1 = bf16[4,2,128,512]{3,2,1,0:T(8,128)(2,1)S(1)} copy-done((bf16[4,2,128,512]{3,2,1,0:T(8,128)(2,1)S(1)}, bf16[4,2,128,512]{3,2,1,0:T(8,128)(2,1)}, u32[]{:S(2)}) %copy-start.1) | copy-done | bytes 1048600
  4.3 0.0 copy-start.2
  4.3 0.9 %copy-done.2 = bf16[4,2,8192]{2,1,0:T(2,128)(2,1)S(1)} copy-done((bf16[4,2,8192]{2,1,0:T(2,128)(2,1)S(1)}, bf16[4,2,8192]{2,1,0:T(2,128)(2,1)}, u32[]{:S(2)}) %copy-start.2) | copy-done | bytes 131096
  5.2 0.0 copy-start.3
  5.2 0.7 %copy-done.3 = bf16[4,2,576]{2,1,0:T(2,128)(2,1)S(1)} copy-done((bf16[4,2,576]{2,1,0:T(2,128)(2,1)S(1)}, bf16[4,2,576]{2,1,0:T(2,128)(2,1)}, u32[]{:S(2)}) %copy-start.3) | copy-done | bytes 9240
  6.0 0.0 copy-start.4
  6.0 0.7 %copy-done.4 = s32[4]{0:T(128)S(1)} copy-done((s32[4]{0:T(128)S(1)}, s32[4]{0:T(128)}, u32[]{:S(2)}) %copy-start.4) | copy-done | bytes 40
  6.6 0.0 copy-start.5
  6.6 0.7 %copy-done.5 = s32[1,2]{1,0:T(1,128)S(1)} copy-done((s32[1,2]{1,0:T(1,128)S(1)}, s32[1,2]{1,0:T(1,128)}, u32[]{:S(2)}) %copy-start.5) | copy-done | bytes 32
  7.3 0.0 copy-start.6
  7.3 0.7 %copy-done.6 = s32[128]{0:T(128)S(1)} copy-done((s32[128]{0:T(128)S(1)}, s32[128]{0:T(128)}, u32[]{:S(2)}) %copy-start.6) | copy-done | bytes 536
  7.9 39.2 %shard_map.82 = bf16[4,32,512]{2,1,0:T(8,128)(2,1)S(1)} custom-call(s32[128]{0:T(128)S(1)} %copy-done.6, s32[4]{0:T(128)S(1)} %copy-done.4, s32[1,2]{1,0:T(1,128)S(1)} %copy-done.5, bf16[4,768,512]{2,1,0:T(8,128)(2,1)S(1)} %bitcast.3, bf16[4,12,4096]{2,1,0:T(8,128)(2,1)S(1)} %copy.9.rope_hbm, bf16[4,2,128,512]{3,2,1,0:T(8,128)(2,1)S(1)} %copy-done.1, ...), custom_call_target="tpu_custom_call" | custom-call | flops 1800000000 | bytes 4800000 | tf_op jit(solution)/shard_map/pallas_call | solution.py:391
  47.1 0.7 %copy.11 = bf16[4,2,16,512]{3,2,1,0:T(8,128)(2,1)} copy(bf16[4,2,16,512]{3,2,1,0:T(8,128)(2,1)S(1)} %bitcast.2) | data formatting | bytes 262144
Async XLA Ops:
  1.2 1.9 %copy-start = (bf16[4,12,64,512]{3,2,1,0:T(8,128)(2,1)S(1)}, bf16[4,12,64,512]{3,2,1,0:T(8,128)(2,1)}, u32[]{:S(2)}) copy-start(bf16[4,12,64,512]{3,2,1,0:T(8,128)(2,1)} %param.8) | copy-start | bytes 9437188
  3.1 1.2 %copy-start.1 = (bf16[4,2,128,512]{3,2,1,0:T(8,128)(2,1)S(1)}, bf16[4,2,128,512]{3,2,1,0:T(8,128)(2,1)}, u32[]{:S(2)}) copy-start(bf16[4,2,128,512]{3,2,1,0:T(8,128)(2,1)} %q_hbm.1) | copy-start | bytes 3145732
  4.3 0.9 %copy-start.2 = (bf16[4,2,8192]{2,1,0:T(2,128)(2,1)S(1)}, bf16[4,2,8192]{2,1,0:T(2,128)(2,1)}, u32[]{:S(2)}) copy-start(bf16[4,2,8192]{2,1,0:T(2,128)(2,1)} %qr_hbm.1) | copy-start | bytes 393220
  5.2 0.7 %copy-start.3 = (bf16[4,2,576]{2,1,0:T(2,128)(2,1)S(1)}, bf16[4,2,576]{2,1,0:T(2,128)(2,1)}, u32[]{:S(2)}) copy-start(bf16[4,2,576]{2,1,0:T(2,128)(2,1)} %nk_hbm.1) | copy-start | bytes 27652
  6.0 0.7 %copy-start.4 = (s32[4]{0:T(128)S(1)}, s32[4]{0:T(128)}, u32[]{:S(2)}) copy-start(s32[4]{0:T(128)} %lengths.1) | copy-start | bytes 52
  6.6 0.7 %copy-start.5 = (s32[1,2]{1,0:T(1,128)S(1)}, s32[1,2]{1,0:T(1,128)}, u32[]{:S(2)}) copy-start(s32[1,2]{1,0:T(1,128)} %moves.1) | copy-start | bytes 28
  7.3 0.7 %copy-start.6 = (s32[128]{0:T(128)S(1)}, s32[128]{0:T(128)}, u32[]{:S(2)}) copy-start(s32[128]{0:T(128)} %constant.2.clone.plan) | copy-start | bytes 1540

commit v2 on v1

v2 whole, which is shorter than its diff:
```python
import functools

import jax
import jax.numpy as jnp
import numpy as np
from jax import lax
from jax.experimental import pallas as pl
from jax.experimental.pallas import tpu as pltpu
from jax.sharding import PartitionSpec as P

score_scale = 192.0 ** (-0.5)
masked = -1e30
MESH = pl.DeviceIdType.MESH
F32 = jnp.float32
BF16 = jnp.bfloat16


def nt(a, b):
    return lax.dot_general(a, b, (((1,), (1,)), ((), ())), preferred_element_type=F32)


def nn(a, b):
    return lax.dot_general(a, b, (((1,), (0,)), ((), ())), preferred_element_type=F32)


def iota(shape, dim):
    return lax.broadcasted_iota(jnp.int32, shape, dim)


def spread_heads(pairs):
    n = pairs.shape[0]
    row, col = iota((2 * n, n), 0), iota((2 * n, n), 1)
    pick = jnp.where(col == (row >> 1), 1.0, 0.0).astype(BF16)
    both = nn(pick, pairs)
    row, lane = iota((2 * n, 128), 0), iota((2 * n, 128), 1)
    one = jnp.where((lane >> 6) == (row & 1), both, 0.0)
    return (one + pltpu.roll(one, 64, 1)).astype(BF16)


def stats_block(top, total):
    lane = iota((top.shape[0], 128), 1)
    block = jnp.zeros((top.shape[0], 128), F32)
    for at, value, terms in ((0, top, 3), (3, total, 2)):
        for n in range(terms):
            term = value.astype(BF16).astype(F32)
            block = jnp.where(lane == at + n, term, block)
            value = value - term
    return block.astype(BF16)


def read_stats(block):
    block = block.astype(F32)
    return block[:, 0:1] + block[:, 1:2] + block[:, 2:3], block[:, 3:4] + block[:, 4:5]


def kernel(
    n_rep,
    tab_hbm,
    len_hbm,
    mov_hbm,
    lat_hbm,
    rope_hbm,
    q_hbm,
    qr_hbm,
    nk_hbm,
    out,
    keys,
    rope_v,
    q_v,
    qown,
    qr_v,
    nk_v,
    xq,
    xk,
    nkx,
    nkf,
    msg,
    nkmsg,
    nkgot,
    qall,
    pages,
    got,
    psend,
    precv,
    own,
    ownstat,
    rs,
    rr,
    newp,
    newstat,
    ysend,
    res,
    tab_s,
    len_s,
    mov_s,
    in_sem,
    y_s,
    y_r,
    ag_s,
    ag_r,
    k_s,
    k_r,
    p_s,
    p_r,
    r_s,
    r_r,
    o_s,
    o_r,
):
    rep = lax.axis_index("rep")
    ctx = lax.axis_index("ctx")
    cx = ctx // 2
    core = ctx % 2
    partner = {"rep": (rep + n_rep // 2) % n_rep, "ctx": ctx}
    other = cx * 2 + (1 - core)
    sibling = {"rep": rep, "ctx": other}

    def chip(d):
        return {"rep": rep, "ctx": ((cx + d) % 4) * 2 + core}

    barrier = pltpu.get_barrier_semaphore()
    for peer in (partner, chip(2), chip(1), chip(3), sibling):
        pl.semaphore_signal(barrier, inc=1, device_id=peer, device_id_type=MESH)

    loads = {}

    def load(name, src, dst):
        copy = pltpu.make_async_copy(src, dst, in_sem.at[len(loads)])
        copy.start()
        loads[name] = copy

    load("plan", tab_hbm, tab_s)
    load("moves", mov_hbm, mov_s)
    load("lengths", len_hbm, len_s)
    load("qr", qr_hbm, qr_v)
    for s in range(2):
        load(("own", s), q_hbm.at[:, s, pl.ds(pl.multiple_of(ctx * 16, 16), 16), :], qown.at[:, s])
    load("nk", nk_hbm, nk_v)
    load("rope", rope_hbm, rope_v)
    for i in range(4):
        load(("lat", i), lat_hbm.at[i], keys.at[i, :, 0:512])
    for g in range(8):
        c = (core + g // 4) % 2
        head = pl.multiple_of(((g % 4) * 2 + c) * 16, 16)
        for s in range(2):
            load(("q", g, s), q_hbm.at[:, s, pl.ds(head, 16), :], q_v.at[:, g, s])

    def remote(src, dst, send_sem, recv_sem, device):
        copy = pltpu.make_async_remote_copy(
            src_ref=src,
            dst_ref=dst,
            send_sem=send_sem,
            recv_sem=recv_sem,
            device_id=device,
            device_id_type=MESH,
        )
        copy.start()
        return copy

    loads["qr"].wait()
    for i in range(4):
        rows = qr_v[i].astype(F32)
        for b in range(64):
            j = b // 8
            at = ((j % 2) * 4 + j // 2) * 16 + b % 8
            for s in range(2):
                xq[i, at + 8 * s : at + 8 * s + 1, :] = rows[s : s + 1, 128 * b : 128 * b + 128]

    for name in ("plan", "lengths", "moves"):
        loads[name].wait()
    row = (mov_s[0, 0] * 4 + mov_s[0, 1]) * 8
    slots = [tab_s[row + i] for i in range(4)]
    places = [tab_s[row + 4 + b] for b in range(4)]

    def pairs_of(slot, c):
        return xq[slot, pl.ds(pl.multiple_of(c * 64, 64), 64), :].astype(BF16)

    def own_pairs(slot):
        return xq[slot, pl.ds(pl.multiple_of(core * 64 + cx * 16, 16), 16), :].astype(BF16)

    for name in (("own", 0), ("own", 1), "nk"):
        loads[name].wait()
    nkx[...] = jnp.zeros_like(nkx)
    for k in range(2):
        slot = slots[2 + k]
        msg[k, :, 0:512] = qown[slot].reshape(32, 512)
        msg[k, :, 512:640] = spread_heads(own_pairs(slot))
        fresh = nk_v[slot].astype(F32)
        for n in range(2):
            for u in range(4):
                nkx[n * 4 + u : n * 4 + u + 1, :] = fresh[n : n + 1, 128 * u : 128 * u + 128]
            nkx[8 + n : 9 + n, 0:64] = fresh[n : n + 1, 512:576]
        nkmsg[k] = nkx[...].astype(BF16)

    def rope_keys():
        loads["rope"].wait()
        for page in range(12):
            rows = rope_v[page].astype(F32)
            for c in range(32):
                for i in range(4):
                    at = page * 32 + c
                    xk[i, at : at + 1, :] = rows[i : i + 1, c * 128 : c * 128 + 128]
        token, col = iota((768, 384), 0), iota((768, 384), 1)
        pick = jnp.where(col == (token >> 1), 1.0, 0.0).astype(BF16)
        token, lane = iota((768, 128), 0), iota((768, 128), 1)
        keep = (lane >> 6) == (token & 1)
        both = nn(pick, jnp.concatenate([xk[i].astype(BF16) for i in range(4)], axis=1))
        for i in range(4):
            keys[i, :, 512:640] = jnp.where(keep, both[:, i * 128 : i * 128 + 128], 0.0).astype(BF16)
        for i in range(4):
            loads[("lat", i)].wait()
        for k in range(2):
            pages[k] = keys[slots[2 + k]]

    def attend(q, held, group, length):
        score = nt(q, held) * score_scale
        valid = group * 768 + iota((1, 768), 1) < length
        score = jnp.where(valid, score, masked)
        top = jnp.max(score, axis=1, keepdims=True)
        weights = jnp.where(valid, jnp.exp(score - top), 0.0)
        total = jnp.sum(weights, axis=1, keepdims=True)
        return nn(weights.astype(BF16), held[:, 0:512]).astype(BF16), top, total

    def stay(i):
        slot = slots[i]
        pairs = jnp.concatenate([pairs_of(slot, core), pairs_of(slot, 1 - core)], axis=0)
        q = jnp.concatenate([q_v[slot].reshape(256, 512), spread_heads(pairs)], axis=1)
        part, top, total = attend(q, keys[slot], ctx, len_s[slot])
        psend[i, :, 0:512] = part[128:256]
        psend[i, :, 512:640] = stats_block(top[128:256], total[128:256])
        own[i] = part[0:128]
        lane = iota((128, 128), 1)
        ownstat[i] = jnp.where(lane == 0, top[0:128], total[0:128])

    def merge(i, a, b):
        part_a, top_a, total_a = a
        part_b, top_b, total_b = b
        top = jnp.maximum(top_a, top_b)
        scale_a, scale_b = jnp.exp(top_a - top), jnp.exp(top_b - top)
        part = scale_a * part_a.astype(F32) + scale_b * part_b.astype(F32)
        rs[i, :, :, 0:512] = part.astype(BF16).reshape(4, 32, 512)
        stats = stats_block(top, scale_a * total_a + scale_b * total_b)
        rs[i, :, :, 512:640] = stats.reshape(4, 32, 128)
        copies = []
        for d in (2, 1, 3):
            src = rs.at[i, (cx + d) % 4]
            copies.append(remote(src, rr.at[i, cx], r_s.at[i, d], r_r.at[i, d], chip(d)))
        rr[i, cx] = rs[i, cx]
        return copies

    def merge_cores(i):
        pairs[i].wait()
        top, total = read_stats(precv[i, :, 512:640])
        return merge(
            i,
            (own[i], ownstat[i, :, 0:1], ownstat[i, :, 1:2]),
            (precv[i, :, 0:512], top, total),
        )

    def merge_chips(i):
        for copy in chips[i]:
            copy.wait()
        blocks = [rr[i, c] for c in range(4)]
        parts = [b[:, 0:512].astype(F32) for b in blocks] + [newp[i]]
        stats = [read_stats(b[:, 512:640]) for b in blocks]
        stats.append((newstat[i, :, 0:1], newstat[i, :, 1:2]))
        top = functools.reduce(jnp.maximum, [t for t, _ in stats])
        factors = [jnp.exp(t - top) for t, _ in stats]
        numer = sum(f * p for f, p in zip(factors, parts))
        denom = sum(f * t for f, (_, t) in zip(factors, stats))
        return (numer / denom).astype(BF16)

    def new_tokens():
        nkf[...] = jnp.zeros_like(nkf)
        for i in range(2):
            nkf[2 * i : 2 * i + 2, 0:576] = nk_v[slots[i]].astype(F32)
        for k in range(2):
            fresh = nkgot[k].astype(F32)
            for n in range(2):
                at = 4 + 2 * k + n
                for u in range(4):
                    nkf[at : at + 1, 128 * u : 128 * u + 128] = fresh[n * 4 + u : n * 4 + u + 1, :]
                nkf[at : at + 1, 512:576] = fresh[8 + n : 9 + n, 0:64]
        fresh = nkf[...].astype(BF16)
        queries = [
            jnp.concatenate([qown[slots[i]].reshape(32, 512), spread_heads(own_pairs(slots[i]))], axis=1)
            for i in range(2)
        ]
        queries = jnp.concatenate(queries + [qall[k, cx] for k in range(2)], axis=0)
        score = nt(queries, fresh) * score_scale
        row, col = iota((128, 128), 0), iota((128, 128), 1)
        valid = ((row >> 5) == (col >> 1)) & ((col & 1) <= ((row >> 4) & 1))
        score = jnp.where(valid, score, masked)
        top = jnp.max(score, axis=1, keepdims=True)
        weights = jnp.where(valid, jnp.exp(score - top), 0.0)
        total = jnp.sum(weights, axis=1, keepdims=True)
        newp[...] = nn(weights.astype(BF16), fresh[:, 0:512]).reshape(4, 32, 512)
        newstat[...] = jnp.where(col == 0, top, total).reshape(4, 32, 128)

    pairs = [None] * 2
    chips = [None] * 4

    rope_keys()
    for g in range(8):
        for s in range(2):
            loads[("q", g, s)].wait()

    pl.semaphore_wait(barrier, 5)
    y_out = [remote(msg.at[k], qall.at[k, cx], y_s.at[k], y_r.at[k], partner) for k in range(2)]
    y_out.append(remote(nkmsg, nkgot, y_s.at[2], y_r.at[2], partner))
    page_out = [remote(pages.at[k], got.at[k], k_s.at[k], k_r.at[k], sibling) for k in range(2)]
    for i in range(2):
        stay(i)
        pairs[i] = remote(psend.at[i], precv.at[i], p_s.at[i], p_r.at[i], sibling)

    gathers = []
    for k in range(2):
        y_out[k].wait_recv()
        for d in (2, 1, 3):
            gathers.append(remote(qall.at[k, cx], qall.at[k, cx], ag_s.at[k, d], ag_r.at[k, d], chip(d)))
    y_out[2].wait_recv()
    new_tokens()

    for k in range(2):
        i, length = 2 + k, len_s[slots[2 + k]]
        page_out[k].wait_recv()
        for copy in gathers[3 * k : 3 * k + 3]:
            copy.wait_recv()
        q = qall[k].reshape(128, 640)
        chips[i] = merge(i, attend(q, pages[k], ctx, length), attend(q, got[k], other, length))
    chips[0] = merge_cores(0)
    chips[1] = merge_cores(1)

    home = []
    for k in range(2):
        ysend[k] = merge_chips(2 + k)
        home.append(remote(ysend.at[k], res.at[2 + k], o_s.at[k], o_r.at[k], partner))
    for i in range(2):
        res[i] = merge_chips(i)

    for copy in y_out + page_out + gathers:
        copy.wait_send()
    for copy in home:
        copy.wait()

    for b in range(4):
        out[b] = res[places[b]]


def plan_table():
    rows = np.zeros((4, 4, 8), np.int32)
    for first in range(4):
        for second in range(4):
            stay = [b for b in range(4) if b not in (first, second)]
            slots = (stay + [first, second])[:4] if first != second else [0, 1, 2, 3]
            rows[first, second, :4] = slots
            rows[first, second, 4:] = [slots.index(b) for b in range(4)]
    return rows.reshape(128)


def body(cache_latent, cache_rope, lengths, move_slots, q_latent, q_rope, new_keys):
    dma = pltpu.SemaphoreType.DMA
    hbm = pl.BlockSpec(memory_space=pltpu.HBM)
    out = pl.pallas_call(
        functools.partial(kernel, lax.axis_size("rep")),
        out_shape=jax.ShapeDtypeStruct((4, 32, 512), BF16),
        in_specs=[hbm] * 8,
        out_specs=pl.BlockSpec(memory_space=pltpu.VMEM),
        scratch_shapes=[
            pltpu.VMEM((4, 768, 640), BF16),
            pltpu.VMEM((12, 4, 4096), BF16),
            pltpu.VMEM((4, 8, 2, 16, 512), BF16),
            pltpu.VMEM((4, 2, 16, 512), BF16),
            pltpu.VMEM((4, 2, 8192), BF16),
            pltpu.VMEM((4, 2, 576), BF16),
            pltpu.VMEM((4, 128, 128), F32),
            pltpu.VMEM((4, 384, 128), F32),
            pltpu.VMEM((16, 128), F32),
            pltpu.VMEM((128, 640), F32),
            pltpu.VMEM((2, 32, 640), BF16),
            pltpu.VMEM((2, 16, 128), BF16),
            pltpu.VMEM((2, 16, 128), BF16),
            pltpu.VMEM((2, 4, 32, 640), BF16),
            pltpu.VMEM((2, 768, 640), BF16),
            pltpu.VMEM((2, 768, 640), BF16),
            pltpu.VMEM((2, 128, 640), BF16),
            pltpu.VMEM((2, 128, 640), BF16),
            pltpu.VMEM((2, 128, 512), BF16),
            pltpu.VMEM((2, 128, 128), F32),
            pltpu.VMEM((4, 4, 32, 640), BF16),
            pltpu.VMEM((4, 4, 32, 640), BF16),
            pltpu.VMEM((4, 32, 512), F32),
            pltpu.VMEM((4, 32, 128), F32),
            pltpu.VMEM((2, 32, 512), BF16),
            pltpu.VMEM((4, 32, 512), BF16),
            pltpu.SMEM((128,), jnp.int32),
            pltpu.SMEM((4,), jnp.int32),
            pltpu.SMEM((1, 2), jnp.int32),
            dma((32,)),
            dma((3,)),
            dma((3,)),
            dma((2, 4)),
            dma((2, 4)),
            dma((2,)),
            dma((2,)),
            dma((2,)),
            dma((2,)),
            dma((4, 4)),
            dma((4, 4)),
            dma((2,)),
            dma((2,)),
        ],
        compiler_params=pltpu.CompilerParams(
            collective_id=0, has_side_effects=True, vmem_limit_bytes=66000000
        ),
        cost_estimate=pl.CostEstimate(flops=1800000000, bytes_accessed=4800000, transcendentals=800000),
    )(
        jnp.asarray(plan_table()),
        lengths,
        move_slots,
        cache_latent.reshape(4, 768, 512),
        cache_rope.transpose(1, 0, 2),
        q_latent,
        q_rope,
        new_keys,
    )
    return out.reshape(4, 2, 16, 512)


def solution(mesh):
    in_specs = (
        P("rep", "ctx", None, None),
        P("rep", "ctx", None),
        P("rep"),
        P("rep", None),
        P("rep", None, None, None),
        P("rep", None, None),
        P("rep", None, None),
    )
    out_specs = P("rep", None, "ctx", None)
    return jax.shard_map(body, mesh=mesh, in_specs=in_specs, out_specs=out_specs, check_vma=False)
```

time: 48.1 us -> 33.8 us (0.70)
  the two profiles are of different devices: /device:TPU:1 before, /device:TPU:392 now
where the time goes in v2:
time: 33.8 us; the launch traced here: 33.7 us
  Pallas kernels  32.1 us (95%)
  local copies, waits for them, and re-layouts  1.57 us (5%)
    pallas_call x1, Pallas kernels, body(): pl.pallas_call(functools.partial(kernel, lax.axis_size('rep')), out_shape...  32.1 us
    unnamed x1, local copies, waits for them, and re-layouts  1.57 us

profile of v2, /device:TPU:392, one launch (start us, length us, event | category | flops | bytes accessed | tf_op | source)
XLA Modules:
  0.0 33.7 jit_solution(12702999571825606141)
XLA Ops:
  0.0 32.1 %shard_map.82 = bf16[4,32,512]{2,1,0:T(8,128)(2,1)} custom-call(s32[128]{0:T(128)} %constant.2.clone.tab_hbm, s32[4]{0:T(128)} %len_hbm.1, s32[1,2]{1,0:T(1,128)} %mov_hbm.1, bf16[4,768,512]{2,1,0:T(8,128)(2,1)} %bitcast.4, bf16[12,4,4096]{2,1,0:T(4,128)(2,1)} %bitcast.5, bf16[4,2,128,512]{3,2,1,0:T(8,128)(2,1)} %q_hbm.1, bf16[4,2,8192]{2,1,0:T(2,128)(2,1)} %qr_hbm.1, ...), custom_call_target="tpu_custom_call" | custom-call | flops 1800000000 | bytes 4800000 | tf_op jit(solution)/shard_map/pallas_call | solution.py:364
  32.1 1.6 %copy.10 = bf16[4,2,16,512]{3,2,1,0:T(8,128)(2,1)} copy(bf16[4,2,16,512]{3,2,1,0:T(8,128)(2,1)} %bitcast.3) | data formatting | bytes 262144

commit v3 on v2

--- a/solution.py
+++ b/solution.py
@@ -80,12 +80,16 @@
     qall,
     pages,
     got,
+    pages_t,
+    got_t,
     psend,
     precv,
     own,
     ownstat,
     rs,
     rr,
+    ms,
+    mr,
     newp,
     newstat,
     ysend,
@@ -104,6 +108,8 @@
     p_r,
     r_s,
     r_r,
+    m_s,
+    m_r,
     o_s,
     o_r,
 ):
@@ -157,6 +163,21 @@
         copy.start()
         return copy
 
+    half = (slice(0, 640), slice(640, 1152))
+    whole = slice(0, 1152)
+    asked = [(k, part) for k in range(2) for part in half]
+    summed = [(k, part) for k in range(2) for part in half]
+
+    def rows_of(block):
+        rot = block[:, 512:640].astype(F32)
+        lane = iota(rot.shape, 1)
+        rots = []
+        for s in range(2):
+            one = jnp.where((lane >> 6) == s, rot, 0.0)
+            rots.append((one + pltpu.roll(one, 64, 1)).astype(BF16))
+        latent = jnp.concatenate([block[:, 0:512], block[:, 640:1152]], axis=0)
+        return jnp.concatenate([latent, jnp.concatenate(rots, axis=0)], axis=1)
+
     loads["qr"].wait()
     for i in range(4):
         rows = qr_v[i].astype(F32)
@@ -183,8 +204,11 @@
     nkx[...] = jnp.zeros_like(nkx)
     for k in range(2):
         slot = slots[2 + k]
-        msg[k, :, 0:512] = qown[slot].reshape(32, 512)
-        msg[k, :, 512:640] = spread_heads(own_pairs(slot))
+        msg[k, :, 0:512] = qown[slot, 0]
+        msg[k, :, 640:1152] = qown[slot, 1]
+        rot = spread_heads(own_pairs(slot))
+        lane = iota((16, 128), 1)
+        msg[k, :, 512:640] = jnp.where(lane < 64, rot[0:16], rot[16:32])
         fresh = nk_v[slot].astype(F32)
         for n in range(2):
             for u in range(4):
@@ -212,8 +236,8 @@
         for k in range(2):
             pages[k] = keys[slots[2 + k]]
 
-    def attend(q, held, group, length):
-        score = nt(q, held) * score_scale
+    def attend(q, held, group, length, turned=None):
+        score = (nt(q, held) if turned is None else nn(q, turned[...])) * score_scale
         valid = group * 768 + iota((1, 768), 1) < length
         score = jnp.where(valid, score, masked)
         top = jnp.max(score, axis=1, keepdims=True)
@@ -232,38 +256,66 @@
         lane = iota((128, 128), 1)
         ownstat[i] = jnp.where(lane == 0, top[0:128], total[0:128])
 
-    def merge(i, a, b):
+    def add(a, b):
         part_a, top_a, total_a = a
         part_b, top_b, total_b = b
         top = jnp.maximum(top_a, top_b)
         scale_a, scale_b = jnp.exp(top_a - top), jnp.exp(top_b - top)
         part = scale_a * part_a.astype(F32) + scale_b * part_b.astype(F32)
-        rs[i, :, :, 0:512] = part.astype(BF16).reshape(4, 32, 512)
-        stats = stats_block(top, scale_a * total_a + scale_b * total_b)
-        rs[i, :, :, 512:640] = stats.reshape(4, 32, 128)
+        return part.astype(BF16), stats_block(top, scale_a * total_a + scale_b * total_b)
+
+    def scatter_stay(i):
+        chips[i] = [
+            remote(rs.at[i, (cx + d) % 4], rr.at[i, cx], r_s.at[i, d], r_r.at[i, d], chip(d))
+            for d in (2, 1, 3)
+        ]
+
+    def scatter_moved(k, total):
+        part, stats = total
+        sent, got = ms.at[k], mr.at[k]
+        for s, at in ((0, slice(0, 512)), (1, slice(640, 1152))):
+            sent[:, :, at] = part[64 * s : 64 * s + 64].reshape(4, 16, 512)
+        lane = iota((64, 128), 1)
+        stats = jnp.where(lane < 64, stats[0:64].astype(F32), pltpu.roll(stats[64:128].astype(F32), 64, 1))
+        sent[:, :, 512:640] = stats.astype(BF16).reshape(4, 16, 128)
         copies = []
-        for d in (2, 1, 3):
-            src = rs.at[i, (cx + d) % 4]
-            copies.append(remote(src, rr.at[i, cx], r_s.at[i, d], r_r.at[i, d], chip(d)))
-        rr[i, cx] = rs[i, cx]
+        for n, (kk, part) in enumerate(summed):
+            if kk == k:
+                copies.append([])
+                for d in (2, 1, 3):
+                    src, dst = sent.at[(cx + d) % 4, :, part], got.at[cx, :, part]
+                    copies[-1].append(remote(src, dst, m_s.at[n, d], m_r.at[n, d], chip(d)))
+        got[cx] = sent[cx]
         return copies
+
+    def merge_moved(k, s):
+        at = slice(0, 512) if s == 0 else slice(640, 1152)
+        here = slice(16 * s, 16 * s + 16)
+        stats = [read_stats(mr[k, c, :, 512 + 64 * s : 640]) for c in range(4)]
+        parts = [mr[k, c, :, at].astype(F32) for c in range(4)]
+        stats.append((newstat[2 + k, here, 0:1], newstat[2 + k, here, 1:2]))
+        parts.append(newp[2 + k, here])
+        return combine(parts, stats)
 
     def merge_cores(i):
         pairs[i].wait()
         top, total = read_stats(precv[i, :, 512:640])
-        return merge(
-            i,
-            (own[i], ownstat[i, :, 0:1], ownstat[i, :, 1:2]),
-            (precv[i, :, 0:512], top, total),
-        )
-
-    def merge_chips(i):
-        for copy in chips[i]:
-            copy.wait()
-        blocks = [rr[i, c] for c in range(4)]
-        parts = [b[:, 0:512].astype(F32) for b in blocks] + [newp[i]]
+        mine = (own[i], ownstat[i, :, 0:1], ownstat[i, :, 1:2])
+        part, stats = add(mine, (precv[i, :, 0:512], top, total))
+        rs[i, :, :, 0:512] = part.reshape(4, 32, 512)
+        rs[i, :, :, 512:640] = stats.reshape(4, 32, 128)
+        rr[i, cx] = rs[i, cx]
+
+    def merge_chips(copies, got, fresh, fresh_stat):
+        for copy in copies:
+            copy.wait_recv()
+        blocks = [got[c] for c in range(4)]
+        parts = [b[:, 0:512].astype(F32) for b in blocks] + [fresh]
         stats = [read_stats(b[:, 512:640]) for b in blocks]
-        stats.append((newstat[i, :, 0:1], newstat[i, :, 1:2]))
+        stats.append((fresh_stat[:, 0:1], fresh_stat[:, 1:2]))
+        return combine(parts, stats)
+
+    def combine(parts, stats):
         top = functools.reduce(jnp.maximum, [t for t, _ in stats])
         factors = [jnp.exp(t - top) for t, _ in stats]
         numer = sum(f * p for f, p in zip(factors, parts))
@@ -286,7 +338,7 @@
             jnp.concatenate([qown[slots[i]].reshape(32, 512), spread_heads(own_pairs(slots[i]))], axis=1)
             for i in range(2)
         ]
-        queries = jnp.concatenate(queries + [qall[k, cx] for k in range(2)], axis=0)
+        queries = jnp.concatenate(queries + [rows_of(qall[k, cx]) for k in range(2)], axis=0)
         score = nt(queries, fresh) * score_scale
         row, col = iota((128, 128), 0), iota((128, 128), 1)
         valid = ((row >> 5) == (col >> 1)) & ((col & 1) <= ((row >> 4) & 1))
@@ -298,47 +350,67 @@
         newstat[...] = jnp.where(col == 0, top, total).reshape(4, 32, 128)
 
     pairs = [None] * 2
-    chips = [None] * 4
+    chips = [None] * 2
 
     rope_keys()
     for g in range(8):
         for s in range(2):
             loads[("q", g, s)].wait()
-
     pl.semaphore_wait(barrier, 5)
-    y_out = [remote(msg.at[k], qall.at[k, cx], y_s.at[k], y_r.at[k], partner) for k in range(2)]
-    y_out.append(remote(nkmsg, nkgot, y_s.at[2], y_r.at[2], partner))
-    page_out = [remote(pages.at[k], got.at[k], k_s.at[k], k_r.at[k], sibling) for k in range(2)]
-    for i in range(2):
+    y_out = []
+    for n, (k, part) in enumerate(asked):
+        src, dst = msg.at[k, :, part], qall.at[k, cx, :, part]
+        y_out.append(remote(src, dst, y_s.at[n], y_r.at[n], partner))
+    y_out.append(remote(nkmsg, nkgot, y_s.at[4], y_r.at[4], partner))
+    for i in (0, 1):
         stay(i)
         pairs[i] = remote(psend.at[i], precv.at[i], p_s.at[i], p_r.at[i], sibling)
-
+    for k in range(2):
+        pages_t[k] = pages[k].T
+    page_out = [remote(pages.at[k, :, 0:512], got.at[k], k_s.at[k], k_r.at[k], sibling) for k in range(2)]
+    turned_out = [remote(pages_t.at[k], got_t.at[k], k_s.at[2 + k], k_r.at[2 + k], sibling) for k in range(2)]
     gathers = []
+    for n, (k, part) in enumerate(asked):
+        y_out[n].wait_recv()
+        block = qall.at[k, cx, :, part]
+        gathers.append([remote(block, block, ag_s.at[n, d], ag_r.at[n, d], chip(d)) for d in (2, 1, 3)])
+    y_out[-1].wait_recv()
+    new_tokens()
+    for i in range(2):
+        merge_cores(i)
+
+    sums = []
     for k in range(2):
-        y_out[k].wait_recv()
-        for d in (2, 1, 3):
-            gathers.append(remote(qall.at[k, cx], qall.at[k, cx], ag_s.at[k, d], ag_r.at[k, d], chip(d)))
-    y_out[2].wait_recv()
-    new_tokens()
-
-    for k in range(2):
-        i, length = 2 + k, len_s[slots[2 + k]]
+        length = len_s[slots[2 + k]]
         page_out[k].wait_recv()
-        for copy in gathers[3 * k : 3 * k + 3]:
-            copy.wait_recv()
-        q = qall[k].reshape(128, 640)
-        chips[i] = merge(i, attend(q, pages[k], ctx, length), attend(q, got[k], other, length))
-    chips[0] = merge_cores(0)
-    chips[1] = merge_cores(1)
+        turned_out[k].wait_recv()
+        for n, (kk, _) in enumerate(asked):
+            if kk == k:
+                for copy in gathers[n]:
+                    copy.wait_recv()
+        q = rows_of(qall[k].reshape(64, 1152))
+        total = add(attend(q, pages[k], ctx, length, pages_t.at[k]), attend(q, got[k], other, length, got_t.at[k]))
+        sums.append(scatter_moved(k, total))
+    scatter_stay(0)
+    scatter_stay(1)
 
     home = []
     for k in range(2):
-        ysend[k] = merge_chips(2 + k)
-        home.append(remote(ysend.at[k], res.at[2 + k], o_s.at[k], o_r.at[k], partner))
+        for s in range(2):
+            if s < len(sums[k]):
+                for copy in sums[k][s]:
+                    copy.wait_recv()
+            at = slice(16 * s, 16 * s + 16)
+            ysend[k, at] = merge_moved(k, s)
+            n = 2 * k + s
+            if 2 == 2:
+                home.append(remote(ysend.at[k, at], res.at[2 + k, at], o_s.at[n], o_r.at[n], partner))
+        if 2 == 1:
+            home.append(remote(ysend.at[k], res.at[2 + k], o_s.at[k], o_r.at[k], partner))
     for i in range(2):
-        res[i] = merge_chips(i)
-
-    for copy in y_out + page_out + gathers:
+        res[i] = merge_chips(chips[i], rr.at[i], newp[i], newstat[i])
+
+    for copy in sum(gathers + sum(sums, []) + chips, y_out + page_out + turned_out):
         copy.wait_send()
     for copy in home:
         copy.wait()
@@ -377,18 +449,22 @@
             pltpu.VMEM((4, 384, 128), F32),
             pltpu.VMEM((16, 128), F32),
             pltpu.VMEM((128, 640), F32),
-            pltpu.VMEM((2, 32, 640), BF16),
+            pltpu.VMEM((2, 16, 1152), BF16),
             pltpu.VMEM((2, 16, 128), BF16),
             pltpu.VMEM((2, 16, 128), BF16),
-            pltpu.VMEM((2, 4, 32, 640), BF16),
+            pltpu.VMEM((2, 4, 16, 1152), BF16),
             pltpu.VMEM((2, 768, 640), BF16),
-            pltpu.VMEM((2, 768, 640), BF16),
+            pltpu.VMEM((2, 768, 512), BF16),
+            pltpu.VMEM((2, 640, 768), BF16),
+            pltpu.VMEM((2, 640, 768), BF16),
             pltpu.VMEM((2, 128, 640), BF16),
             pltpu.VMEM((2, 128, 640), BF16),
             pltpu.VMEM((2, 128, 512), BF16),
             pltpu.VMEM((2, 128, 128), F32),
-            pltpu.VMEM((4, 4, 32, 640), BF16),
-            pltpu.VMEM((4, 4, 32, 640), BF16),
+            pltpu.VMEM((2, 4, 32, 640), BF16),
+            pltpu.VMEM((2, 4, 32, 640), BF16),
+            pltpu.VMEM((2, 4, 16, 1152), BF16),
+            pltpu.VMEM((2, 4, 16, 1152), BF16),
             pltpu.VMEM((4, 32, 512), F32),
             pltpu.VMEM((4, 32, 128), F32),
             pltpu.VMEM((2, 32, 512), BF16),
@@ -397,32 +473,39 @@
             pltpu.SMEM((4,), jnp.int32),
             pltpu.SMEM((1, 2), jnp.int32),
             dma((32,)),
-            dma((3,)),
-            dma((3,)),
+            dma((5,)),
+            dma((5,)),
+            dma((4, 4)),
+            dma((4, 4)),
+            dma((4,)),
+            dma((4,)),
+            dma((2,)),
+            dma((2,)),
             dma((2, 4)),
             dma((2, 4)),
-            dma((2,)),
-            dma((2,)),
-            dma((2,)),
-            dma((2,)),
             dma((4, 4)),
             dma((4, 4)),
-            dma((2,)),
-            dma((2,)),
+            dma((4,)),
+            dma((4,)),
         ],
         compiler_params=pltpu.CompilerParams(
-            collective_id=0, has_side_effects=True, vmem_limit_bytes=66000000
+            collective_id=0, has_side_effects=True, vmem_limit_bytes=48 * 1024 * 1024
         ),
         cost_estimate=pl.CostEstimate(flops=1800000000, bytes_accessed=4800000, transcendentals=800000),
     )(
-        jnp.asarray(plan_table()),
-        lengths,
-        move_slots,
-        cache_latent.reshape(4, 768, 512),
-        cache_rope.transpose(1, 0, 2),
-        q_latent,
-        q_rope,
-        new_keys,
+        *[
+            pltpu.with_memory_space_constraint(x, pltpu.HBM)
+            for x in (
+                jnp.asarray(plan_table()),
+                lengths,
+                move_slots,
+                cache_latent.reshape(4, 768, 512),
+                cache_rope.transpose(1, 0, 2),
+                q_latent,
+                q_rope,
+                new_keys,
+            )
+        ]
     )
     return out.reshape(4, 2, 16, 512)
 

time: 33.8 us -> 31.3 us (0.926)
  the two profiles are of different devices: /device:TPU:392 before, /device:TPU:2 now
where the time goes in v3:
time: 31.3 us; the launch traced here: 31.2 us
  Pallas kernels  30.5 us (97%)
  local copies, waits for them, and re-layouts  0.66 us (2%)
    pallas_call x1, Pallas kernels, body(): pl.pallas_call(functools.partial(kernel, lax.axis_size('rep')), out_shape...  30.5 us
    unnamed x1, local copies, waits for them, and re-layouts  0.66 us

profile of v3, /device:TPU:2, one launch (start us, length us, event | category | flops | bytes accessed | tf_op | source)
XLA Modules:
  0.0 31.2 jit_solution(4314378346967130038)
XLA Ops:
  0.0 30.5 %shard_map.82 = bf16[4,32,512]{2,1,0:T(8,128)(2,1)S(1)} custom-call(s32[128]{0:T(128)} %constant.2.clone.tab_hbm, s32[4]{0:T(128)} %len_hbm.1, s32[1,2]{1,0:T(1,128)} %mov_hbm.1, bf16[4,768,512]{2,1,0:T(8,128)(2,1)} %bitcast.4, bf16[12,4,4096]{2,1,0:T(4,128)(2,1)} %bitcast.5, bf16[4,2,128,512]{3,2,1,0:T(8,128)(2,1)} %q_hbm.1, bf16[4,2,8192]{2,1,0:T(2,128)(2,1)} %qr_hbm.1, ...), custom_call_target="tpu_custom_call" | custom-call | flops 1800000000 | bytes 4800000 | tf_op jit(solution)/shard_map/pallas_call | solution.py:436
  30.5 0.7 %copy.10 = bf16[4,2,16,512]{3,2,1,0:T(8,128)(2,1)} copy(bf16[4,2,16,512]{3,2,1,0:T(8,128)(2,1)S(1)} %bitcast.3) | data formatting | bytes 262144

commit v4 on v3

--- a/solution.py
+++ b/solution.py
@@ -369,6 +369,9 @@
         pages_t[k] = pages[k].T
     page_out = [remote(pages.at[k, :, 0:512], got.at[k], k_s.at[k], k_r.at[k], sibling) for k in range(2)]
     turned_out = [remote(pages_t.at[k], got_t.at[k], k_s.at[2 + k], k_r.at[2 + k], sibling) for k in range(2)]
+    for i in range(2):
+        merge_cores(i)
+    scatter_stay(0)
     gathers = []
     for n, (k, part) in enumerate(asked):
         y_out[n].wait_recv()
@@ -376,8 +379,6 @@
         gathers.append([remote(block, block, ag_s.at[n, d], ag_r.at[n, d], chip(d)) for d in (2, 1, 3)])
     y_out[-1].wait_recv()
     new_tokens()
-    for i in range(2):
-        merge_cores(i)
 
     sums = []
     for k in range(2):
@@ -391,8 +392,6 @@
         q = rows_of(qall[k].reshape(64, 1152))
         total = add(attend(q, pages[k], ctx, length, pages_t.at[k]), attend(q, got[k], other, length, got_t.at[k]))
         sums.append(scatter_moved(k, total))
-    scatter_stay(0)
-    scatter_stay(1)
 
     home = []
     for k in range(2):
@@ -407,6 +406,7 @@
                 home.append(remote(ysend.at[k, at], res.at[2 + k, at], o_s.at[n], o_r.at[n], partner))
         if 2 == 1:
             home.append(remote(ysend.at[k], res.at[2 + k], o_s.at[k], o_r.at[k], partner))
+    scatter_stay(1)
     for i in range(2):
         res[i] = merge_chips(chips[i], rr.at[i], newp[i], newstat[i])
 

time: 31.3 us -> 32.1 us (1.026)
  the two profiles are of different devices: /device:TPU:2 before, /device:TPU:1 now
where the time goes in v4:
time: 32.1 us; the launch traced here: 32 us
  Pallas kernels  31.3 us (98%)
  local copies, waits for them, and re-layouts  0.66 us (2%)
    pallas_call x1, Pallas kernels, body(): pl.pallas_call(functools.partial(kernel, lax.axis_size('rep')), out_shape...  31.3 us
    unnamed x1, local copies, waits for them, and re-layouts  0.66 us

profile of v4, /device:TPU:1, one launch (start us, length us, event | category | flops | bytes accessed | tf_op | source)
XLA Modules:
  0.0 32.0 jit_solution(15493389211759919048)
XLA Ops:
  0.0 31.3 %shard_map.82 = bf16[4,32,512]{2,1,0:T(8,128)(2,1)S(1)} custom-call(s32[128]{0:T(128)} %constant.2.clone.tab_hbm, s32[4]{0:T(128)} %len_hbm.1, s32[1,2]{1,0:T(1,128)} %mov_hbm.1, bf16[4,768,512]{2,1,0:T(8,128)(2,1)} %bitcast.4, bf16[12,4,4096]{2,1,0:T(4,128)(2,1)} %bitcast.5, bf16[4,2,128,512]{3,2,1,0:T(8,128)(2,1)} %q_hbm.1, bf16[4,2,8192]{2,1,0:T(2,128)(2,1)} %qr_hbm.1, ...), custom_call_target="tpu_custom_call" | custom-call | flops 1800000000 | bytes 4800000 | tf_op jit(solution)/shard_map/pallas_call | solution.py:436
  31.3 0.7 %copy.10 = bf16[4,2,16,512]{3,2,1,0:T(8,128)(2,1)} copy(bf16[4,2,16,512]{3,2,1,0:T(8,128)(2,1)S(1)} %bitcast.3) | data formatting | bytes 262144
